TPU v7x, 128 devices: a whole 4x4x4 slice. The times are simulated.
128 devices in a mesh: segment: 4 (over x), seq: 32 (over z, y, core).
Axes of the slice: x: 4, y: 4, z: 4, core: 2. Of those that a mesh axis runs over, the one named last changes fastest.
Arguments:
- hidden: bfloat16 [4, 32768, 8192], P('segment', 'seq'), may hold values from -6 to 6
- span_lengths: int32 [4, 256], replicated, may hold values from 1 to 512, 32768 in all within a row
- section_of: int32 [4, 256], replicated, may hold values from 0 to 127
- section_live: int32 [128], P('seq'), may hold values 0 or 1
- w_in: bfloat16 [8192, 2048], P('seq'), may hold values from -0.5 to 0.5
- norm_gain: float32 [2048], replicated, may hold values from 0.5 to 1.5
- w_query: bfloat16 [2048, 2048], P(None, 'segment'), may hold values from -0.125 to 0.125
- w_key: bfloat16 [2048, 2048], P(None, 'segment'), may hold values from -0.125 to 0.125
- w_value: bfloat16 [2048, 2048], P(None, 'segment'), may hold values from -0.125 to 0.125
- w_out: bfloat16 [2048, 2048], P('segment'), may hold values from -0.125 to 0.125
Outputs:
- section_out: bfloat16 [128, 2048], P('seq')
All inputs are finite; a program needn't handle non-finite values. No bound on the sum of `section_live` on one device may be relied on, other than what follows from the above.
Results may differ from a plain program's by a relative error of at most 0.007.
Values may be sent and summed in bfloat16 or wider, within the bound.
No kernel may reach another device: no remote copies, remote signals or barrier semaphores. Data moves between devices by JAX's collectives and lax.ppermute only.
A program may use at most 128 MiB of HBM per device.

v0:
```python
import jax
import jax.numpy as jnp
from jax import lax
from jax.sharding import PartitionSpec as P

HEAD_DIM = 128


def shards(
    hidden, span_lengths, section_of, section_live, w_in, norm_gain, w_query, w_key, w_value, w_out
):
    tokens = hidden[0]
    seq_count = lax.axis_size("seq")
    seq_index = lax.axis_index("seq")
    segment_index = lax.axis_index("segment")
    tok_count = tokens.shape[0]
    lengths = lax.dynamic_index_in_dim(span_lengths, segment_index, 0, keepdims=False)
    span_ends = jnp.cumsum(lengths)
    span_starts = span_ends - lengths
    positions = seq_index * tok_count + jnp.arange(tok_count, dtype=jnp.int32)
    member = (
        (positions[None, :] >= span_starts[:, None]) & (positions[None, :] < span_ends[:, None])
    ).astype(jnp.bfloat16)
    partial_value = jnp.dot(member, tokens, preferred_element_type=jnp.float32)
    length_float = lengths.astype(jnp.float32)
    sections_here = section_live.shape[0]
    section_total = sections_here * seq_count
    section_ids = jnp.arange(section_total, dtype=jnp.int32)
    own_sections = seq_index * sections_here + jnp.arange(sections_here, dtype=jnp.int32)
    flat_sections = section_of.reshape(-1)
    count_all = jnp.sum(
        (section_ids[:, None] == flat_sections[None, :]).astype(jnp.float32), axis=1
    )
    doc_sections = lax.dynamic_index_in_dim(section_of, segment_index, 0, keepdims=False)
    feature_block = lax.psum_scatter(partial_value, "seq", scatter_dimension=1, tiled=True)
    span_means = feature_block / length_float[:, None]
    doc_onehot = (section_ids[:, None] == doc_sections[None, :]).astype(jnp.float32)
    section_part = jnp.dot(doc_onehot, span_means, precision=lax.Precision.HIGHEST)
    doc_total = lax.psum(section_part, "segment")
    pooled = (doc_total / jnp.maximum(count_all, 1.0)[:, None]).astype(jnp.bfloat16)
    projected = jnp.dot(pooled, w_in, preferred_element_type=jnp.float32)
    section_in = lax.psum_scatter(projected, "seq", scatter_dimension=0, tiled=True)
    scale = lax.rsqrt(jnp.mean(section_in * section_in, axis=1, keepdims=True) + 1e-05)
    normed = (section_in * scale * norm_gain[None, :]).astype(jnp.bfloat16)
    queries = jnp.dot(normed, w_query, preferred_element_type=jnp.float32).astype(jnp.bfloat16)
    keys_here = jnp.dot(normed, w_key, preferred_element_type=jnp.float32).astype(jnp.bfloat16)
    values_here = jnp.dot(normed, w_value, preferred_element_type=jnp.float32).astype(jnp.bfloat16)
    live_here = section_live.astype(jnp.bfloat16)
    keys_all, values_all, live_all = (
        lax.all_gather(keys_here, "seq", axis=0, tiled=True),
        lax.all_gather(values_here, "seq", axis=0, tiled=True),
        lax.all_gather(live_here, "seq", axis=0, tiled=True),
    )
    local_heads = queries.shape[1] // HEAD_DIM
    query_heads = queries.reshape(sections_here, local_heads, HEAD_DIM)
    key_heads = keys_all.reshape(section_total, local_heads, HEAD_DIM)
    value_heads = values_all.reshape(section_total, local_heads, HEAD_DIM)
    scores = jnp.einsum("qhd,khd->hqk", query_heads, key_heads, preferred_element_type=jnp.float32)
    scores = scores / jnp.sqrt(jnp.float32(HEAD_DIM))
    allowed = (live_all[None, :] > 0) | (section_ids[None, :] == own_sections[:, None])
    scores = jnp.where(allowed[None, :, :], scores, jnp.float32(-1e30))
    probs = jax.nn.softmax(scores, axis=-1).astype(jnp.bfloat16)
    attended = jnp.einsum(
        "hqk,khd->qhd", probs, value_heads, preferred_element_type=jnp.float32
    ).astype(jnp.bfloat16)
    attended = attended.reshape(sections_here, local_heads * HEAD_DIM)
    head_terms = jnp.dot(attended, w_out, preferred_element_type=jnp.float32)
    combined = lax.psum(head_terms, "segment")
    return (section_in + combined).astype(jnp.bfloat16)


def solution(mesh):
    in_specs = (
        P("segment", "seq", None),
        P(),
        P(),
        P("seq"),
        P("seq", None),
        P(),
        P(None, "segment"),
        P(None, "segment"),
        P(None, "segment"),
        P("segment", None),
    )
    out_specs = P("seq", None)
    return jax.shard_map(shards, mesh=mesh, in_specs=in_specs, out_specs=out_specs, check_vma=False)
```

profile of v0, /device:TPU:0, one launch (start us, length us, event | category | flops | bytes accessed | tf_op | source)
XLA Modules:
  0.0 347.7 jit_solution(3386403767242706925)
XLA Ops:
  6.5 0.0 copy-start
  6.5 0.0 reduce-scatter.2.cloned.1.call-start
  6.5 0.8 constant_dynamic-slice_fusion
  7.4 0.3 reduce-window.9
  7.7 0.1 slice.7
  7.8 0.1 slice_reduce_fusion
  7.9 0.1 fusion.29
  8.0 12.6 %fusion.1 = f32[256,8192]{1,0:T(8,128)} fusion(bf16[1,1024,8192]{2,1,0:T(8,128)(2,1)} %param.10, s32[1024]{0:T(1024)S(1)} %iota_add_fusion, s32[256]{0:T(256)S(1)} %get-tuple-element.6, s32[256]{0:T(256)S(1)} %get-tuple-element.5), kind=kOutput, calls=%fused_computation.1 | convolution fusion | flops 4295753728 | bytes 25171968 | tf_op jit(solution)/shard_map/dot_general | solution.py:24
  20.6 0.0 copy-start.3
  20.6 0.0 copy-start.5
  20.6 0.0 copy-start.4
  20.6 0.0 copy-start.1
  20.6 0.0 reduce-scatter.2.cloned.1.call-update
  20.6 0.0 all-reduce.5.cloned.1.call-start
  20.7 0.6 copy-done.3
  21.3 0.0 copy-done.5
  21.3 0.0 copy-done.4
  21.3 0.6 fusion.30
  23.2 0.2 dynamic-update-slice
  23.5 69.4 %all-reduce = bf16[128]{0:T(256)(128)(2,1)S(1)} all-reduce(bf16[128]{0:T(256)(128)(2,1)S(1)} %dynamic-update-slice), channel_id=1, replica_groups=mesh['segment'=4,'seq'=32] {'seq'}, use_global_device_ids=true, to_apply=%add | all-reduce | flops 128 | bytes 512
  92.9 0.1 convert_reduce_fusion
  93.0 23.1 %reduce-scatter.2.cloned.1.call-done = f32[256,256]{1,0:T(8,128)} async-done(((f32[256,8192]{1,0:T(8,128)}), f32[256,256]{1,0:T(8,128)}) %reduce-scatter.2.cloned.1.call-update) | async-done | bytes 262160 | tf_op jit(solution)/shard_map/reduce_scatter | solution.py:35
  116.1 0.0 copy-start.2
  116.1 1.9 fusion.17
  118.1 0.0 all-reduce.5.cloned.1.call-update
  118.1 0.0 all-reduce.7.cloned.1.call-start
  118.1 40.8 %all-reduce.5.cloned.1.call-done = f32[128,256]{1,0:T(8,128)} async-done(((f32[128,256]{1,0:T(8,128)}), f32[128,256]{1,0:T(8,128)}) %all-reduce.5.cloned.1.call-update) | async-done | bytes 131088 | tf_op jit(solution)/shard_map/psum | solution.py:39
  158.9 0.0 copy-done.1
  158.9 2.3 fusion.23
  161.2 0.0 all-reduce.7.cloned.1.call-update
  161.2 0.1 fusion.28
  161.3 106.5 %all-reduce.7.cloned.1.call-done = f32[128,2048]{1,0:T(8,128)} async-done(((f32[128,2048]{1,0:T(8,128)}), f32[128,2048]{1,0:T(8,128)}) %all-reduce.7.cloned.1.call-update) | async-done | bytes 1048592
  267.8 1.0 multiply_reduce_fusion
  268.7 0.0 copy-done.2
  268.7 2.0 fusion.8
  270.8 25.0 %all-gather.1 = bf16[32,4,512]{2,1,0:T(4,128)(2,1)S(1)} all-gather(bf16[1,4,512]{2,1,0:T(4,128)(2,1)S(1)} %fusion.8), channel_id=1, replica_groups=mesh['segment'=4,'seq'=32] {'seq'}, dimensions={0}, use_global_device_ids=true | all-gather | bytes 135168 | tf_op jit(solution)/shard_map/all_gather | solution.py:50
  295.8 0.1 reshape.118
  295.9 2.2 fusion.5
  298.0 0.2 fusion.31
  298.2 2.1 fusion.6
  300.3 21.8 %all-gather = bf16[32,4,512]{2,1,0:T(4,128)(2,1)S(1)} all-gather(bf16[1,4,512]{2,1,0:T(4,128)(2,1)S(1)} %fusion.6), channel_id=1, replica_groups=mesh['segment'=4,'seq'=32] {'seq'}, dimensions={0}, use_global_device_ids=true | all-gather | bytes 135168 | tf_op jit(solution)/shard_map/all_gather | solution.py:51
  322.1 0.1 reshape.116
  322.2 0.0 copy-done
  322.2 0.5 fusion.13
  322.7 17.0 %psum.15 = f32[4,2048]{1,0:T(4,128)S(1)} all-reduce(f32[4,2048]{1,0:T(4,128)S(1)} %fusion.13), channel_id=1, replica_groups=mesh['segment'=4,'seq'=32] {'segment'}, use_global_device_ids=true, to_apply=%region_9.10 | all-reduce | flops 8192 | bytes 65536 | tf_op jit(solution)/shard_map/psum | solution.py:68
  339.7 1.5 add_convert_fusion
  (11 shorter events, 0.1 us)
Async XLA Ops:
  6.5 315.6 %copy-start = (bf16[512,2048]{1,0:T(8,128)(2,1)S(1)}, bf16[512,2048]{1,0:T(8,128)(2,1)}, u32[]{:S(2)}) copy-start(bf16[512,2048]{1,0:T(8,128)(2,1)} %param.19) | copy-start | bytes 6291460
  6.5 109.6 %reduce-scatter.2.cloned.1.call-start = ((), (), s32[]{:S(2)}) async-start(), calls=%async_computation.1 | async-start | bytes 8650752 | tf_op jit(solution)/shard_map/reduce_scatter | solution.py:35
  20.6 0.7 copy-start.3
  20.6 0.7 copy-start.5
  20.6 0.7 copy-start.4
  20.6 138.3 %copy-start.1 = (bf16[256,2048]{1,0:T(8,128)(2,1)S(1)}, bf16[256,2048]{1,0:T(8,128)(2,1)}, u32[]{:S(2)}) copy-start(bf16[256,2048]{1,0:T(8,128)(2,1)} %param.14) | copy-start | bytes 3145732
  20.6 138.3 %all-reduce.5.cloned.1.call-start = ((), (), s32[]{:S(2)}) async-start(), calls=%async_computation.2 | async-start | bytes 262144 | tf_op jit(solution)/shard_map/psum | solution.py:39
  116.1 152.6 %copy-start.2 = (f32[2048]{0:T(1024)S(1)}, f32[2048]{0:T(1024)}, u32[]{:S(2)}) copy-start(f32[2048]{0:T(1024)} %param.15) | copy-start | bytes 24580
  118.1 149.7 %all-reduce.7.cloned.1.call-start = ((), (), s32[]{:S(2)}) async-start(), calls=%async_computation.3 | async-start | bytes 2097152
Sparse Core Ops, SparseCore 0:
  20.8 95.2 reduce-scatter.1
  118.5 40.3 all-reduce.4
  162.1 105.5 all-reduce.6
where the time goes:
time: 348 us
  waiting for transfers between devices  170 us (49%)
  blocking collectives  133 us (38%)
  matrix products  23.7 us (7%)
  between operations  14.5 us (4%)
    unnamed x4, waiting for transfers between devices  107 us
    unnamed x1, blocking collectives  69.4 us
    psum x1, waiting for transfers between devices, shards(): doc_total = lax.psum(section_part, 'segment')  40.8 us
    all_gather x1, blocking collectives, shards(): lax.all_gather(keys_here, 'seq', axis=0, tiled=True)  25 us
    reduce_scatter x1, waiting for transfers between devices, shards(): lax.psum_scatter(partial_value, 'seq', scatter_dimension=1, tiled=True)  23.1 us
    all_gather x1, blocking collectives, shards(): lax.all_gather(values_here, 'seq', axis=0, tiled=True)  21.8 us
    psum x1, blocking collectives, shards(): combined = lax.psum(head_terms, 'segment')  17 us
    dot_general x1, matrix products, shards(): partial_value = jnp.dot(member, tokens, preferred_element_type=jnp.float32)  12.6 us
  transfers between devices with their start and end apart: 3, of which 3 were waited for; matrix products, arithmetic and copies ran while one was open for 0% of the time, Pallas kernels for 0%

commit v1 on v0

v1 whole, which is shorter than its diff:
```python
import functools

import jax
import jax.numpy as jnp
from jax import lax
from jax.experimental import pallas as pl
from jax.experimental.pallas import tpu as pltpu
from jax.sharding import PartitionSpec as P

HEAD_DIM = 128
SLOTS = 32
F32 = jnp.float32
BF16 = jnp.bfloat16
I32 = jnp.int32


def iota(shape, dim):
    return lax.broadcasted_iota(I32, shape, dim)


def column_of(row):
    count = row.shape[1]
    same = iota((count, count), 0) == iota((count, count), 1)
    return jnp.sum(jnp.where(same, row, 0), axis=1, keepdims=True)


def pool_kernel(
    slots, peers, chunks, hidden, lens, secs, rows, place, most, buf, sems
):
    docs, spans = lens.shape
    toks, width = buf.shape
    step = width // chunks
    copies = [
        pltpu.make_async_copy(
            hidden.at[0, :, pl.ds(j * step, step)], buf.at[:, pl.ds(j * step, step)], sems.at[j]
        )
        for j in range(chunks)
    ]
    for copy in copies:
        copy.start()
    doc = lax.axis_index("segment")
    here = lax.axis_index("seq")
    tok0 = here * toks

    def pick(ref):
        return jnp.sum(jnp.where(iota((docs, spans), 0) == doc, ref[...], 0), axis=0, keepdims=True)

    len_row = pick(lens)
    sec_row = pick(secs)
    len_col = column_of(len_row)
    sec_col = column_of(sec_row)
    upto = iota((spans, spans), 0) <= iota((spans, spans), 1)
    end_row = jnp.sum(jnp.where(upto, len_col, 0), axis=0, keepdims=True)
    end_col = column_of(end_row)
    first = jnp.sum((end_row <= tok0).astype(I32), axis=1, keepdims=True)
    mine = iota((slots, spans), 1) == iota((slots, spans), 0) + first

    def slot(row):
        return jnp.sum(jnp.where(mine, row, 0), axis=1, keepdims=True)

    stop = slot(end_row)
    length = slot(len_row)
    section = slot(sec_row)
    count = jnp.zeros((slots, 1), F32)
    for d in range(docs):
        count = count + jnp.sum((secs[d : d + 1, :] == section).astype(F32), axis=1, keepdims=True)
    at = tok0 + iota((slots, toks), 1)
    member = ((at >= stop - length) & (at < stop)).astype(BF16)
    per_len = 1.0 / jnp.maximum(length, 1).astype(F32)
    per_count = 1.0 / jnp.maximum(count, 1.0)

    peer_width = width // peers
    for j in range(chunks):
        copies[j].wait()
        part = jnp.dot(member, buf[:, j * step : (j + 1) * step], preferred_element_type=F32)
        part = (part * per_len * per_count).astype(BF16)
        for i in range(step // peer_width):
            rows[j * (step // peer_width) + i] = part[:, i * peer_width : (i + 1) * peer_width]

    total = place.shape[1]
    lanes = 1024

    @pl.loop(0, total // lanes)
    def _(block):
        r = block * lanes + iota((1, lanes), 1)
        owner = r // slots
        begin = jnp.sum((end_col <= owner * toks).astype(I32), axis=0, keepdims=True)
        span = begin + (r - owner * slots)
        sec = jnp.sum(jnp.where(iota((spans, 1), 0) == span, sec_col, 0), axis=0, keepdims=True)
        hit = (iota((place.shape[0], 1), 0) == sec).astype(F32).astype(BF16)
        place[:, pl.ds(pl.multiple_of(block * lanes, lanes), lanes)] = hit

    worst = jnp.zeros((1, 1), I32)
    low = iota((1, 128), 1) * toks
    for d in range(docs):
        lcol = column_of(lens[d : d + 1, :])
        erow = jnp.sum(jnp.where(upto, lcol, 0), axis=0, keepdims=True)
        ecol = column_of(erow)
        held = jnp.sum(
            ((ecol > low) & (ecol - lcol < low + toks)).astype(I32), axis=0, keepdims=True
        )
        worst = jnp.maximum(worst, jnp.max(held, axis=1, keepdims=True))
    most[0, 0] = jnp.max(worst)


def pool(hidden, span_lengths, section_of, slots, peers, sections):
    toks, width = hidden.shape[1:]
    chunks = 16
    return pl.pallas_call(
        functools.partial(pool_kernel, slots, peers, chunks),
        out_shape=(
            jax.ShapeDtypeStruct((peers, slots, width // peers), BF16),
            jax.ShapeDtypeStruct((sections, peers * slots), BF16),
            jax.ShapeDtypeStruct((1, 1), I32),
        ),
        in_specs=[
            pl.BlockSpec(memory_space=pl.ANY),
            pl.BlockSpec(memory_space=pltpu.VMEM),
            pl.BlockSpec(memory_space=pltpu.VMEM),
        ],
        out_specs=(
            pl.BlockSpec(memory_space=pltpu.VMEM),
            pl.BlockSpec(memory_space=pltpu.VMEM),
            pl.BlockSpec(memory_space=pltpu.SMEM),
        ),
        scratch_shapes=[
            pltpu.VMEM((toks, width), BF16),
            pltpu.SemaphoreType.DMA((chunks,)),
        ],
        compiler_params=pltpu.CompilerParams(vmem_limit_bytes=48 * 1024 * 1024),
        name="pool",
    )(hidden, span_lengths, section_of)


def regroup(rows, place):
    got = lax.all_to_all(rows, "seq", 0, 0, tiled=True)
    got = got.reshape(-1, got.shape[-1])
    return jnp.dot(place, got, preferred_element_type=F32).astype(BF16)


def spread(block, axis):
    size = lax.axis_size(axis)
    return lax.all_to_all(jnp.broadcast_to(block[None], (size,) + block.shape), axis, 0, 0, tiled=True)


def shards(
    hidden, span_lengths, section_of, section_live, w_in, norm_gain, w_query, w_key, w_value, w_out
):
    peers = lax.axis_size("seq")
    seq_index = lax.axis_index("seq")
    sections_here = section_live.shape[0]
    sections = sections_here * peers
    spans = span_lengths.shape[1]
    rows, place, most = pool(hidden, span_lengths, section_of, SLOTS, peers, sections)

    def few(_):
        return regroup(rows, place)

    def many(_):
        all_rows, all_place, _ = pool(hidden, span_lengths, section_of, spans, peers, sections)
        return regroup(all_rows, all_place)

    pooled = lax.cond(most[0, 0] <= SLOTS, few, many, 0)
    projected = jnp.dot(pooled, w_in, preferred_element_type=F32).astype(BF16)
    projected = lax.all_to_all(
        projected.reshape(peers, sections_here, -1), "seq", 0, 0, tiled=True
    )
    doc_in = jnp.sum(projected.astype(F32), axis=0)
    section_in = jnp.sum(spread(doc_in, "segment"), axis=0)
    scale = lax.rsqrt(jnp.mean(section_in * section_in, axis=1, keepdims=True) + 1e-05)
    normed = (section_in * scale * norm_gain[None, :]).astype(BF16)
    keys_here = jnp.dot(normed, w_key, preferred_element_type=F32).astype(BF16)
    values_here = jnp.dot(normed, w_value, preferred_element_type=F32).astype(BF16)
    cols = keys_here.shape[1]
    live_here = jnp.broadcast_to(section_live[:, None], (sections_here, 128)).astype(BF16)
    packed = spread(jnp.concatenate([keys_here, values_here, live_here], axis=1), "seq")
    queries = jnp.dot(normed, w_query, preferred_element_type=F32).astype(BF16)
    packed = packed.reshape(sections, -1)
    keys_all, values_all, live_all = (
        packed[:, :cols],
        packed[:, cols : 2 * cols],
        packed[:, 2 * cols],
    )
    heads = cols // HEAD_DIM
    query_heads = queries.reshape(sections_here, heads, HEAD_DIM)
    key_heads = keys_all.reshape(sections, heads, HEAD_DIM)
    value_heads = values_all.reshape(sections, heads, HEAD_DIM)
    scores = jnp.einsum("qhd,khd->hqk", query_heads, key_heads, preferred_element_type=F32)
    scores = scores / jnp.sqrt(F32(HEAD_DIM))
    own = seq_index * sections_here + jnp.arange(sections_here, dtype=I32)
    allowed = (live_all[None, :] > 0) | (jnp.arange(sections, dtype=I32)[None, :] == own[:, None])
    scores = jnp.where(allowed[None, :, :], scores, F32(-1e30))
    probs = jax.nn.softmax(scores, axis=-1).astype(BF16)
    attended = jnp.einsum("hqk,khd->qhd", probs, value_heads, preferred_element_type=F32)
    attended = attended.astype(BF16).reshape(sections_here, cols)
    terms = jnp.dot(attended, w_out, preferred_element_type=F32)
    combined = jnp.sum(spread(terms, "segment"), axis=0)
    return (section_in + combined).astype(BF16)


def solution(mesh):
    in_specs = (
        P("segment", "seq", None),
        P(),
        P(),
        P("seq"),
        P("seq", None),
        P(),
        P(None, "segment"),
        P(None, "segment"),
        P(None, "segment"),
        P("segment", None),
    )
    return jax.shard_map(
        shards, mesh=mesh, in_specs=in_specs, out_specs=P("seq", None), check_vma=False
    )
```

time: 348 us -> 88.1 us (0.25)
  waiting for transfers between devices: 170 us -> 15.2 us
  blocking collectives: 133 us -> 43.6 us
  matrix products: 23.7 us -> 6.91 us
  between operations: 14.5 us -> 0.81 us
  Pallas kernels: 0 us -> 9.13 us
  starting transfers between devices: 0.09 us -> 8.16 us
    unnamed x4 -> x0, waiting for transfers between devices: 107 us -> none
    unnamed x1 -> x0, blocking collectives: 69.4 us -> none
    all_gather x2 -> x0, blocking collectives: 46.8 us -> none  [the longest x1 25 us: shards(): lax.all_gather(keys_here, 'seq', axis=0, tiled=True)]
    all_to_all x0 -> x3, blocking collectives: none -> 43.6 us  [the longest x1 20 us: regroup(): got = lax.all_to_all(rows, 'seq', 0, 0, tiled=True)]
    psum x1 -> x0, waiting for transfers between devices: 40.8 us -> none  [shards(): doc_total = lax.psum(section_part, 'segment')]
    reduce_scatter x1 -> x0, waiting for transfers between devices: 23.1 us -> none  [shards(): lax.psum_scatter(partial_value, 'seq', scatter_dimension=1, tiled=True)]
    psum x1 -> x0, blocking collectives: 17 us -> none  [shards(): combined = lax.psum(head_terms, 'segment')]
    dot_general x6 -> x5, matrix products: 21.5 us -> 4.81 us  [the longest x1 2.08 us: shards(): jnp.dot(normed, w_value, preferred_element_type=F32).astype(BF16)]
  transfers between devices with their start and end apart: 3 -> 2, of which waited for: 3 -> 2; matrix products, arithmetic and copies ran while one was open for 0% -> 0% of each run, Pallas kernels for 0% -> 0%
where the time goes in v1:
time: 88.1 us; the launch traced here: 87.6 us
  blocking collectives  43.6 us (49%)
  waiting for transfers between devices  15.2 us (17%)
  Pallas kernels  9.13 us (10%)
  starting transfers between devices  8.16 us (9%)
  matrix products  6.91 us (8%)
  local copies, waits for them, and re-layouts  2.11 us (2%)
  other arithmetic  1.49 us (2%)
    all_to_all x1, blocking collectives, regroup(): got = lax.all_to_all(rows, 'seq', 0, 0, tiled=True)  20 us
    all_to_all x1, blocking collectives, shards(): lax.all_to_all(projected.reshape(peers, sections_here, -1), 'seq', 0, 0,...  15.2 us
    all_to_all x2, waiting for transfers between devices, spread(): lax.all_to_all(jnp.broadcast_to(block[None], (size,) + block.shape), axis...  15.2 us
    pallas_call x1, Pallas kernels, pool(): pl.pallas_call(functools.partial(pool_kernel, slots, peers, chunks), out_...  9.13 us
    all_to_all x1, blocking collectives, spread(): lax.all_to_all(jnp.broadcast_to(block[None], (size,) + block.shape), axis...  8.36 us
    all_to_all x2, starting transfers between devices, spread(): lax.all_to_all(jnp.broadcast_to(block[None], (size,) + block.shape), axis...  8.16 us
    dot_general x1, matrix products, shards(): jnp.einsum('qhd,khd->hqk', query_heads, key_heads, preferred_element_type...  2.1 us
    dot_general x1, matrix products, shards(): jnp.dot(normed, w_value, preferred_element_type=F32).astype(BF16)  2.08 us
  transfers between devices with their start and end apart: 2, of which 2 were waited for; matrix products, arithmetic and copies ran while one was open for 0% of the time, Pallas kernels for 0%

profile of v1, /device:TPU:0, one launch (start us, length us, event | category | flops | bytes accessed | tf_op | source)
XLA Modules:
  0.0 87.6 jit_solution(5933135277243806905)
XLA Ops:
  0.0 0.0 copy-start
  0.0 0.0 copy-start.2
  0.0 0.0 copy-start.3
  0.0 9.1 %pool.3 = (bf16[32,32,256]{2,1,0:T(8,128)(2,1)S(1)}, bf16[128,1024]{1,0:T(8,128)(2,1)S(1)}, s32[1,1]{1,0:T(1,128)}) custom-call(bf16[1,1024,8192]{2,1,0:T(8,128)(2,1)} %hidden.1, s32[4,256]{1,0:T(4,128)} %lens.1, s32[4,256]{1,0:T(4,128)} %secs.1), custom_call_target="tpu_custom_call" | custom-call | tf_op jit(solution)/shard_map/pool/pallas_call | solution.py:109
  9.8 0.0 copy-done.2
  9.8 0.0 copy-done.3
  9.8 20.4 %conditional.2 = (bf16[128,256]{1,0:T(8,128)(2,1)S(1)}) conditional(s32[]{:T(128)} %bitcast.2, (bf16[1,1024,8192]{2,1,0:T(8,128)(2,1)}, s32[4,256]{1,0:T(4,128)S(1)}, s32[4,256]{1,0:T(4,128)S(1)}) %tuple.20, (bf16[32,32,256]{2,1,0:T(8,128)(2,1)S(1)}, bf16[128,1024]{1,0:T(8,128)(2,1)S(1)}) %tuple.15), branch_computations={%region_0.0_spmd, %region_1.0_spmd} | conditional | flops 536870912 | bytes 14745608
  9.8 20.0 %all_to_all.29 = bf16[32,32,256]{2,1,0:T(8,128)(2,1)S(1)} all-to-all(bf16[32,32,256]{2,1,0:T(8,128)(2,1)S(1)} %get-tuple-element.26), channel_id=1, replica_groups=mesh['segment'=4,'seq'=32] {'seq'}, dimensions={0} | all-to-all | bytes 1048576 | tf_op jit(solution)/shard_map/cond/branch_1_fun/all_to_all | solution.py:136
  29.8 0.2 fusion.14
  30.2 0.0 copy-start.5
  30.3 0.0 copy-start.4
  30.3 1.5 %convolution_convert_fusion = bf16[128,2048]{1,0:T(8,128)(2,1)S(1)} fusion(bf16[256,2048]{1,0:T(8,128)(2,1)} %param.16, bf16[128,256]{1,0:T(8,128)(2,1)S(1)} %get-tuple-element.35), kind=kOutput, calls=%fused_computation.1 | convolution fusion | flops 134479872 | bytes 1638400 | tf_op jit(solution)/shard_map/dot_general | solution.py:164
  31.8 0.2 reshape.90
  32.0 15.2 %all_to_all.30 = bf16[32,4,2048]{2,1,0:T(4,128)(2,1)S(1)} all-to-all(bf16[32,4,2048]{2,1,0:T(4,128)(2,1)S(1)} %reshape.90), channel_id=1, replica_groups=mesh['segment'=4,'seq'=32] {'seq'}, dimensions={0} | all-to-all | bytes 1048576 | tf_op jit(solution)/shard_map/all_to_all | solution.py:165
  47.2 0.2 convert_reduce_fusion
  47.5 0.7 broadcast_in_dim.16
  48.1 4.3 %all-to-all-start.3 = ((f32[4,4,2048]{2,1,0:T(4,128)}), f32[4,4,2048]{2,1,0:T(4,128)S(1)}, u32[]{:S(2)}, u32[]{:S(2)}) async-start(f32[4,4,2048]{2,1,0:T(4,128)} %broadcast_in_dim.16), calls=%async_computation.3 | async-start | bytes 262144 | tf_op jit(solution)/shard_map/all_to_all | solution.py:143
  52.4 0.0 copy-done.5
  52.4 6.0 %all-to-all-done.3 = f32[4,4,2048]{2,1,0:T(4,128)S(1)} async-done(((f32[4,4,2048]{2,1,0:T(4,128)}), f32[4,4,2048]{2,1,0:T(4,128)S(1)}, u32[]{:S(2)}, u32[]{:S(2)}) %all-to-all-start.3) | async-done | bytes 131104 | tf_op jit(solution)/shard_map/all_to_all | solution.py:143
  58.4 0.0 copy-start.1
  58.4 0.1 multiply_reduce_fusion
  58.6 0.0 copy-done.4
  58.6 0.1 multiply_convert_fusion
  58.7 2.1 %convolution_convert_fusion.3 = bf16[4,512]{1,0:T(4,128)(2,1)S(1)} fusion(bf16[4,2048]{1,0:T(4,128)(2,1)S(1)} %multiply_convert_fusion, bf16[2048,512]{1,0:T(8,128)(2,1)} %param.20), kind=kOutput, calls=%fused_computation.8 | convolution fusion | flops 8390656 | bytes 2117632 | tf_op jit(solution)/shard_map/dot_general | solution.py:173
  60.7 0.0 copy-done.1
  60.7 0.4 convolution_convert_fusion.4
  61.1 0.1 broadcast_in_dim.17
  61.2 0.8 broadcast_in_dim.18
  62.0 3.9 %all-to-all-start.4 = ((bf16[32,4,1152]{2,1,0:T(4,128)(2,1)}), bf16[32,4,1152]{2,1,0:T(4,128)(2,1)S(1)}, u32[]{:S(2)}, u32[]{:S(2)}) async-start(bf16[32,4,1152]{2,1,0:T(4,128)(2,1)} %broadcast_in_dim.18), calls=%async_computation.4 | async-start | bytes 589824 | tf_op jit(solution)/shard_map/all_to_all | solution.py:143
  65.9 9.2 %all-to-all-done.4 = bf16[32,4,1152]{2,1,0:T(4,128)(2,1)S(1)} async-done(((bf16[32,4,1152]{2,1,0:T(4,128)(2,1)}), bf16[32,4,1152]{2,1,0:T(4,128)(2,1)S(1)}, u32[]{:S(2)}, u32[]{:S(2)}) %all-to-all-start.4) | async-done | bytes 294944 | tf_op jit(solution)/shard_map/all_to_all | solution.py:143
  75.2 0.1 reshape.91
  75.3 0.1 compare_reduce_fusion
  75.4 0.1 copy.23
  75.5 0.1 copy.24
  75.6 0.1 fusion.10
  75.7 2.1 %fusion.3 = f32[4,4,128]{2,1,0:T(4,128)S(1)} fusion(bf16[128,4,128]{0,2,1:T(8,128)(2,1)S(1)} %bitcast.34, bf16[4,2048]{1,0:T(4,128)(2,1)S(1)} %multiply_convert_fusion, bf16[2048,512]{1,0:T(8,128)(2,1)} %param.18, pred[4,128]{1,0:T(4,128)(4,1)S(1)} %fusion.10), kind=kOutput, calls=%fused_computation.5 | convolution fusion | flops 8919040 | bytes 2253312 | tf_op jit(solution)/shard_map/qhd,khd->hqk/dot_general | solution.py:188
  77.8 0.2 fusion.12
  78.0 0.0 copy-done
  78.0 0.6 fusion.6
  78.6 8.4 %all_to_all.31 = f32[4,4,2048]{2,1,0:T(4,128)S(1)} all-to-all(f32[4,4,2048]{2,1,0:T(4,128)S(1)} %broadcast_in_dim.25), channel_id=1, replica_groups=mesh['segment'=4,'seq'=32] {'segment'}, dimensions={0} | all-to-all | bytes 262144 | tf_op jit(solution)/shard_map/all_to_all | solution.py:143
  87.0 0.6 add_convert_fusion
  (8 shorter events, 0.1 us)
Async XLA Ops:
  0.0 78.0 %copy-start = (bf16[512,2048]{1,0:T(8,128)(2,1)S(1)}, bf16[512,2048]{1,0:T(8,128)(2,1)}, u32[]{:S(2)}) copy-start(bf16[512,2048]{1,0:T(8,128)(2,1)} %param.21) | copy-start | bytes 6291460
  0.0 9.8 %copy-start.2 = (s32[4,256]{1,0:T(4,128)S(1)}, s32[4,256]{1,0:T(4,128)}, u32[]{:S(2)}) copy-start(s32[4,256]{1,0:T(4,128)} %lens.1) | copy-start | bytes 12292
  0.0 9.8 %copy-start.3 = (s32[4,256]{1,0:T(4,128)S(1)}, s32[4,256]{1,0:T(4,128)}, u32[]{:S(2)}) copy-start(s32[4,256]{1,0:T(4,128)} %secs.1) | copy-start | bytes 12292
  30.2 22.2 %copy-start.5 = (s32[4]{0:T(128)S(1)}, s32[4]{0:T(128)}, u32[]{:S(2)}) copy-start(s32[4]{0:T(128)} %param.15) | copy-start | bytes 52
  30.3 28.3 %copy-start.4 = (f32[2048]{0:T(1024)S(1)}, f32[2048]{0:T(1024)}, u32[]{:S(2)}) copy-start(f32[2048]{0:T(1024)} %param.17) | copy-start | bytes 24580
  48.1 10.3 %all-to-all-start.3 = ((f32[4,4,2048]{2,1,0:T(4,128)}), f32[4,4,2048]{2,1,0:T(4,128)S(1)}, u32[]{:S(2)}, u32[]{:S(2)}) async-start(f32[4,4,2048]{2,1,0:T(4,128)} %broadcast_in_dim.16), calls=%async_computation.3 | async-start | bytes 262144 | tf_op jit(solution)/shard_map/all_to_all | solution.py:143
  58.4 2.3 %copy-start.1 = (bf16[2048,512]{1,0:T(8,128)(2,1)S(1)}, bf16[2048,512]{1,0:T(8,128)(2,1)}, u32[]{:S(2)}) copy-start(bf16[2048,512]{1,0:T(8,128)(2,1)} %param.19) | copy-start | bytes 6291460
  62.0 13.1 %all-to-all-start.4 = ((bf16[32,4,1152]{2,1,0:T(4,128)(2,1)}), bf16[32,4,1152]{2,1,0:T(4,128)(2,1)S(1)}, u32[]{:S(2)}, u32[]{:S(2)}) async-start(bf16[32,4,1152]{2,1,0:T(4,128)(2,1)} %broadcast_in_dim.18), calls=%async_computation.4 | async-start | bytes 589824 | tf_op jit(solution)/shard_map/all_to_all | solution.py:143

commit v2 on v0

v2 whole, which is shorter than its diff:
```python
import functools

import jax
import jax.numpy as jnp
from jax import lax
from jax.experimental import pallas as pl
from jax.experimental.pallas import tpu as pltpu
from jax.sharding import PartitionSpec as P

HEAD_DIM = 128
SLOTS = 16
DEAD = 2.0**100
F32 = jnp.float32
BF16 = jnp.bfloat16
I32 = jnp.int32


def iota(shape, dim):
    return lax.broadcasted_iota(I32, shape, dim)


def below(shape, dim, other):
    return (iota(shape, dim) < iota(shape, other)).astype(F32).astype(BF16)


def turn(row):
    count = row.shape[1]
    same = iota((count, count), 0) == iota((count, count), 1)
    return jnp.sum(jnp.where(same, row, 0), axis=1, keepdims=True)


def turn_back(col):
    count = col.shape[0]
    same = iota((count, count), 0) == iota((count, count), 1)
    return jnp.sum(jnp.where(same, col, 0), axis=0, keepdims=True)


def pool_kernel(groups, slots, peers, chunks, hidden, lens, secs, *refs):
    rows, places, (level, buf, sems) = refs[:groups], refs[groups : 2 * groups], refs[2 * groups :]
    docs, spans = lens.shape
    sections = places[0].shape[-1]
    toks, width = buf.shape
    step = width // chunks
    copies = [
        pltpu.make_async_copy(
            hidden.at[0, :, pl.ds(j * step, step)], buf.at[:, pl.ds(j * step, step)], sems.at[j]
        )
        for j in range(chunks)
    ]
    for copy in copies:
        copy.start()
    doc = lax.axis_index("segment")
    here = lax.axis_index("seq")
    tok0 = (here * toks).astype(F32)
    lengths = lens[...]
    high = (lengths >> 4).astype(F32).astype(BF16)
    low = (lengths & 15).astype(F32).astype(BF16)
    upto = (iota((spans, spans), 0) <= iota((spans, spans), 1)).astype(F32).astype(BF16)
    ends = 16.0 * jnp.dot(high, upto, preferred_element_type=F32)
    ends = ends + jnp.dot(low, upto, preferred_element_type=F32)
    starts = ends - lengths.astype(F32)

    def pick(values):
        own = iota((docs, spans), 0) == doc
        return jnp.sum(jnp.where(own, values, 0), axis=0, keepdims=True)

    end_row = pick(ends)
    start_row = pick(starts)
    sec_row = pick(secs[...])
    section = iota((sections, 1), 0)
    hits = [section == secs[d : d + 1, :] for d in range(docs)]
    count = sum(hit.astype(F32) for hit in hits)
    count = jnp.sum(count, axis=1, keepdims=True)
    own = section == sec_row
    cover = (start_row < tok0 + toks) & (end_row > tok0)
    present = jnp.max((own & cover).astype(F32), axis=1, keepdims=True)
    ahead = iota((sections, sections), 1) < iota((sections, sections), 0)
    rank = jnp.sum(jnp.where(ahead, turn_back(present), 0.0), axis=1, keepdims=True)
    count_row = jnp.sum(jnp.where(own, count, 0.0), axis=0, keepdims=True)
    slot_row = jnp.sum(jnp.where(own, rank, 0.0), axis=0, keepdims=True)
    weight = 1.0 / jnp.maximum((end_row - start_row) * count_row, 1.0)
    every = groups * slots
    chosen = jnp.where(slot_row == iota((every, spans), 0).astype(F32), weight, 0.0)
    coarse = chosen.astype(BF16)
    fine = (chosen - coarse.astype(F32)).astype(BF16)
    at = tok0 + iota((1, toks), 1).astype(F32)
    inside = (turn(start_row) <= at) & (turn(end_row) > at)
    inside = inside.astype(F32).astype(BF16)
    picked = jnp.dot(jnp.concatenate([coarse, fine], axis=0), inside, preferred_element_type=F32)
    picked = picked.astype(BF16)

    peer_width = width // peers

    def work(j):
        copies[j].wait()
        part = jnp.dot(picked, buf[:, j * step : (j + 1) * step], preferred_element_type=F32)
        part = (part[:every] + part[every:]).astype(BF16)
        for i in range(step // peer_width):
            block = part[:, i * peer_width : (i + 1) * peer_width]
            for g in range(groups):
                rows[g][j * (step // peer_width) + i] = block[g * slots : (g + 1) * slots]

    for j in range(chunks // 2):
        work(j)

    edge = (iota((peers, 1), 0) * toks).astype(F32)
    before = below((sections, sections), 0, 1)

    def seen(start, end, hit):
        cover = ((start < edge + toks) & (end > edge)).astype(F32).astype(BF16)
        hit = hit.astype(F32).astype(BF16)
        found = lax.dot_general(cover, hit, (((1,), (1,)), ((), ())), preferred_element_type=F32)
        return (found > 0.0).astype(F32)

    mine = seen(start_row, end_row, own)
    order = jnp.dot(mine.astype(BF16), before, preferred_element_type=F32)
    order = jnp.where(mine > 0.0, order, -1.0)
    for q in range(peers):
        for g in range(groups):
            spot = (iota((slots, sections), 0) + g * slots).astype(F32)
            places[g][q] = (order[q : q + 1, :] == spot).astype(F32).astype(BF16)
    worst = jnp.zeros((peers, 1), F32)
    for d in range(docs):
        held = seen(starts[d : d + 1, :], ends[d : d + 1, :], hits[d])
        worst = jnp.maximum(worst, jnp.sum(held, axis=1, keepdims=True))
    worst = jnp.max(worst)
    level[0, 0] = (worst > slots).astype(I32) + (worst > 2 * slots).astype(I32)

    for j in range(chunks // 2, chunks):
        work(j)


def pool(hidden, span_lengths, section_of, groups, slots, peers, sections):
    toks, width = hidden.shape[1:]
    chunks = 16
    vmem = pl.BlockSpec(memory_space=pltpu.VMEM)
    out = pl.pallas_call(
        functools.partial(pool_kernel, groups, slots, peers, chunks),
        out_shape=(
            *[jax.ShapeDtypeStruct((peers, slots, width // peers), BF16)] * groups,
            *[jax.ShapeDtypeStruct((peers, slots, sections), BF16)] * groups,
            jax.ShapeDtypeStruct((1, 1), I32),
        ),
        in_specs=[pl.BlockSpec(memory_space=pl.ANY), vmem, vmem],
        out_specs=(*[vmem] * (2 * groups), pl.BlockSpec(memory_space=pltpu.SMEM)),
        scratch_shapes=[pltpu.VMEM((toks, width), BF16), pltpu.SemaphoreType.DMA((chunks,))],
        compiler_params=pltpu.CompilerParams(vmem_limit_bytes=50 * 1024 * 1024),
        name="pool",
    )(hidden, span_lengths, section_of)
    return out[:groups], out[groups : 2 * groups], out[-1]


def regroup(rows, place):
    got = lax.all_to_all(rows, "seq", 0, 0, tiled=True)
    got = got.reshape(-1, got.shape[-1])
    place = place.reshape(-1, place.shape[-1])
    pooled = lax.dot_general(place, got, (((0,), (0,)), ((), ())), preferred_element_type=F32)
    return pooled.astype(BF16)


def from_segments(block):
    size = lax.axis_size("segment")
    others = [
        lax.ppermute(block, "segment", [(i, (i + k) % size) for i in range(size)])
        for k in range(1, size)
    ]
    return [block, *others]


def project_kernel(pooled, w_in, _, out, wide):
    here = out.shape[1]
    wide[...] = jnp.dot(pooled[...], w_in[...], preferred_element_type=F32)
    for q in range(out.shape[0]):
        out[q] = wide[q * here : (q + 1) * here, :].astype(BF16)


def project(pooled, w_in, ahead, peers):
    sections, width = pooled.shape[0], w_in.shape[1]
    vmem = pl.BlockSpec(memory_space=pltpu.VMEM)
    return pl.pallas_call(
        project_kernel,
        out_shape=jax.ShapeDtypeStruct((peers, sections // peers, width), BF16),
        in_specs=[vmem] * 3,
        out_specs=vmem,
        scratch_shapes=[pltpu.VMEM((sections, width), F32)],
        compiler_params=pltpu.CompilerParams(vmem_limit_bytes=24 * 1024 * 1024),
        name="project",
    )(pooled, w_in, ahead)


def add_kernel(got, _, out):
    total = got[0].astype(F32)
    for q in range(1, got.shape[0]):
        total = total + got[q].astype(F32)
    out[...] = total


def add_peers(got, ahead):
    vmem = pl.BlockSpec(memory_space=pltpu.VMEM)
    return pl.pallas_call(
        add_kernel,
        out_shape=jax.ShapeDtypeStruct(got.shape[1:], F32),
        in_specs=[vmem] * 2,
        out_specs=vmem,
        compiler_params=pltpu.CompilerParams(vmem_limit_bytes=24 * 1024 * 1024),
        name="add_peers",
    )(got, ahead)


def by_head(full, here):
    row = iota((full.shape[0], 1), 0) // here
    heads = full.shape[0] // here
    return sum(
        jnp.where(row == h, full[:, h * HEAD_DIM : (h + 1) * HEAD_DIM], 0.0) for h in range(heads)
    )


def keys_kernel(docs, *refs):
    got, refs = refs[:docs], refs[docs:]
    gain, w_query, w_key, w_value, live, section_in, query, own, sent, wide = refs
    here = got[0].shape[0]
    heads = w_query.shape[1] // HEAD_DIM
    total = got[0][...]
    for part in got[1:]:
        total = total + part[...]
    section_in[...] = total
    scale = lax.rsqrt(jnp.mean(total * total, axis=1, keepdims=True) + 1e-05)
    normed = total * scale * gain[...]
    for h in range(heads):
        wide[h * here : (h + 1) * here, :] = normed
    normed = wide[...].astype(BF16)

    def project(weight):
        full = jnp.dot(normed, weight[...], preferred_element_type=F32)
        return by_head(full, here)

    key = project(w_key)
    value = project(w_value)
    spot = lax.rem(iota((heads * here, 1), 0), here)
    alive = jnp.zeros((heads * here, 1), I32)
    for i in range(here):
        alive = jnp.where(spot == i, live[i], alive)
    alive = alive > 0
    flag = jnp.where(iota(key.shape, 1) == 0, F32(DEAD), 0.0)
    pair = jnp.concatenate([jnp.where(alive, key, flag), jnp.where(alive, value, 0.0)], axis=1)
    pair = pair.astype(BF16)
    for q in range(sent.shape[0]):
        sent[q] = pair
    own[...] = jnp.concatenate([key, value], axis=1).astype(BF16)
    query[...] = project(w_query).astype(BF16)


def attend_kernel(got, query, own, w_out, terms, wide):
    peers, rows, _ = got.shape
    here = terms.shape[0]
    heads = rows // here
    both = got[...].reshape(peers * rows, 2 * HEAD_DIM)
    keys, values = both[:, :HEAD_DIM], both[:, HEAD_DIM:]
    across = (((1,), (1,)), ((), ()))
    q = query[...]
    root = jnp.sqrt(F32(HEAD_DIM))
    scores = lax.dot_general(q, keys, across, preferred_element_type=F32) / root
    first = (iota(q.shape, 1) == 0).astype(F32).astype(BF16)
    mark = lax.dot_general(first, keys, across, preferred_element_type=F32)
    mine_key = own[:, :HEAD_DIM].astype(F32)
    mine_value = own[:, HEAD_DIM:].astype(F32)
    score = jnp.sum(q.astype(F32) * mine_key, axis=1, keepdims=True) / root
    lane = iota((1, peers * rows), 1)
    row = iota((rows, 1), 0)
    mine = lane == row + lax.axis_index("seq") * rows
    same = lax.rem(lane, rows) // here == row // here
    scores = jnp.where(mark > DEAD * 0.5, F32(-1e30), scores)
    scores = jnp.where(mine, score, scores)
    peak = jnp.max(jnp.where(same, scores, F32(-3e38)), axis=1, keepdims=True)
    probs = jnp.where(same, jnp.exp(scores - peak), 0.0)
    probs = (probs / jnp.sum(probs, axis=1, keepdims=True)).astype(BF16).astype(F32)
    alone = jnp.sum(jnp.where(mine, probs, 0.0), axis=1, keepdims=True)
    rest = jnp.where(mine, 0.0, probs).astype(BF16)
    attended = jnp.dot(rest, values, preferred_element_type=F32) + alone * mine_value
    spread_out = jnp.concatenate([attended] * heads, axis=1)
    block = iota((1, heads * HEAD_DIM), 1) // HEAD_DIM
    spread_out = jnp.where(block == row // here, spread_out, 0.0).astype(BF16)
    wide[...] = jnp.dot(spread_out, w_out[...], preferred_element_type=F32)
    term = wide[0:here, :]
    for h in range(1, heads):
        term = term + wide[h * here : (h + 1) * here, :]
    terms[...] = term


def make_keys(got, gain, w_query, w_key, w_value, live, peers):
    here, width = got[0].shape
    rows = w_query.shape[1] // HEAD_DIM * here
    vmem = pl.BlockSpec(memory_space=pltpu.VMEM)
    return pl.pallas_call(
        functools.partial(keys_kernel, len(got)),
        out_shape=(
            jax.ShapeDtypeStruct((here, width), F32),
            jax.ShapeDtypeStruct((rows, HEAD_DIM), BF16),
            jax.ShapeDtypeStruct((rows, 2 * HEAD_DIM), BF16),
            jax.ShapeDtypeStruct((peers, rows, 2 * HEAD_DIM), BF16),
        ),
        in_specs=[vmem] * (len(got) + 4) + [pl.BlockSpec(memory_space=pltpu.SMEM)],
        out_specs=(vmem,) * 4,
        scratch_shapes=[pltpu.VMEM((rows, width), F32)],
        compiler_params=pltpu.CompilerParams(vmem_limit_bytes=24 * 1024 * 1024),
        name="make_keys",
    )(*got, gain[None, :], w_query, w_key, w_value, live)


def attend(got, query, own, w_out, here):
    rows, width = query.shape[0], w_out.shape[1]
    vmem = pl.BlockSpec(memory_space=pltpu.VMEM)
    return pl.pallas_call(
        attend_kernel,
        out_shape=jax.ShapeDtypeStruct((here, width), F32),
        in_specs=[vmem] * 4,
        out_specs=vmem,
        scratch_shapes=[pltpu.VMEM((rows, width), F32)],
        compiler_params=pltpu.CompilerParams(vmem_limit_bytes=24 * 1024 * 1024),
        name="attend",
    )(got, query, own, w_out)


def shards(
    hidden, span_lengths, section_of, section_live, w_in, norm_gain, w_query, w_key, w_value, w_out
):
    peers = lax.axis_size("seq")
    sections_here = section_live.shape[0]
    sections = sections_here * peers
    rows, place, level = pool(hidden, span_lengths, section_of, 2, SLOTS, peers, sections)

    def few(_):
        return regroup(rows[0], place[0])

    def some(_):
        return regroup(jnp.concatenate(rows, axis=1), jnp.concatenate(place, axis=1))

    def many(_):
        all_rows, all_place, _ = pool(
            hidden, span_lengths, section_of, 1, sections, peers, sections
        )
        return regroup(all_rows[0], all_place[0])

    pooled = lax.switch(level[0, 0], (few, some, many), 0)
    projected = project(pooled, w_in, w_query, peers)
    projected = lax.all_to_all(projected, "seq", 0, 0, tiled=True)
    doc_in = add_peers(projected, w_key)
    section_in, query, own, sent = make_keys(
        from_segments(doc_in), norm_gain, w_query, w_key, w_value, section_live, peers
    )
    got = lax.all_to_all(sent, "seq", 0, 0, tiled=True)
    terms = attend(got, query, own, w_out, sections_here)
    combined = sum(from_segments(terms))
    return (section_in + combined).astype(BF16)


def solution(mesh):
    in_specs = (
        P("segment", "seq", None),
        P(),
        P(),
        P("seq"),
        P("seq", None),
        P(),
        P(None, "segment"),
        P(None, "segment"),
        P(None, "segment"),
        P("segment", None),
    )
    return jax.shard_map(
        shards, mesh=mesh, in_specs=in_specs, out_specs=P("seq", None), check_vma=False
    )
```

time: 348 us -> 73.5 us (0.21)
  waiting for transfers between devices: 170 us -> 8.16 us
  blocking collectives: 133 us -> 45.3 us
  matrix products: 23.7 us -> 0.23 us
  between operations: 14.5 us -> 0.78 us
  Pallas kernels: 0 us -> 10.6 us
  starting transfers between devices: 0.09 us -> 7.53 us
    unnamed x4 -> x0, waiting for transfers between devices: 107 us -> none
    unnamed x1 -> x0, blocking collectives: 69.4 us -> none
    all_gather x2 -> x0, blocking collectives: 46.8 us -> none  [the longest x1 25 us: shards(): lax.all_gather(keys_here, 'seq', axis=0, tiled=True)]
    all_to_all x0 -> x3, blocking collectives: none -> 45.3 us  [the longest x1 17.4 us: regroup(): got = lax.all_to_all(rows, 'seq', 0, 0, tiled=True)]
    psum x1 -> x0, waiting for transfers between devices: 40.8 us -> none  [shards(): doc_total = lax.psum(section_part, 'segment')]
    dot_general x7 -> x1, matrix products: 23.7 us -> 0.23 us  [regroup(): lax.dot_general(place, got, (((0,), (0,)), ((), ())), preferred_element_t...]
    reduce_scatter x1 -> x0, waiting for transfers between devices: 23.1 us -> none  [shards(): lax.psum_scatter(partial_value, 'seq', scatter_dimension=1, tiled=True)]
    psum x1 -> x0, blocking collectives: 17 us -> none  [shards(): combined = lax.psum(head_terms, 'segment')]
  transfers between devices with their start and end apart: 3 -> 6, of which waited for: 3 -> 6; matrix products, arithmetic and copies ran while one was open for 0% -> 0% of each run, Pallas kernels for 0% -> 0%
where the time goes in v2:
time: 73.5 us; the launch traced here: 73.3 us
  blocking collectives  45.3 us (62%)
  Pallas kernels  10.6 us (14%)
  waiting for transfers between devices  8.16 us (11%)
  starting transfers between devices  7.53 us (10%)
  between operations  0.78 us (1%)
    all_to_all x1, blocking collectives, regroup(): got = lax.all_to_all(rows, 'seq', 0, 0, tiled=True)  17.4 us
    all_to_all x1, blocking collectives, shards(): projected = lax.all_to_all(projected, 'seq', 0, 0, tiled=True)  15.6 us
    all_to_all x1, blocking collectives, shards(): got = lax.all_to_all(sent, 'seq', 0, 0, tiled=True)  12.4 us
    ppermute x6, waiting for transfers between devices, from_segments(): lax.ppermute(block, 'segment', [(i, (i + k) % size) for i in range(size)])  8.16 us
    pallas_call x1, Pallas kernels, pool(): pl.pallas_call(functools.partial(pool_kernel, groups, slots, peers, chunk...  7.68 us
    ppermute x6, starting transfers between devices, from_segments(): lax.ppermute(block, 'segment', [(i, (i + k) % size) for i in range(size)])  7.53 us
    pallas_call x1, Pallas kernels, make_keys(): pl.pallas_call(functools.partial(keys_kernel, len(got)), out_shape=(jax.S...  1.56 us
  transfers between devices with their start and end apart: 6, of which 6 were waited for; matrix products, arithmetic and copies ran while one was open for 0% of the time, Pallas kernels for 0%

profile of v2, /device:TPU:0, one launch (start us, length us, event | category | flops | bytes accessed | tf_op | source)
XLA Modules:
  0.0 73.3 jit_solution(14382171437013737791)
XLA Ops:
  0.0 0.0 copy-start.7
  0.0 0.0 copy-start.8
  0.0 7.7 %pool.3 = (bf16[32,16,256]{2,1,0:T(8,128)(2,1)S(1)}, bf16[32,16,256]{2,1,0:T(8,128)(2,1)S(1)}, bf16[32,16,128]{2,1,0:T(8,128)(2,1)S(1)}, bf16[32,16,128]{2,1,0:T(8,128)(2,1)S(1)}, s32[1,1]{1,0:T(1,128)}) custom-call(bf16[1,1024,8192]{2,1,0:T(8,128)(2,1)} %hidden.1, s32[4,256]{1,0:T(4,128)} %lens.1, s32[4,256]{1,0:T(4,128)} %secs.1), custom_call_target="tpu_custom_call" | custom-call | tf_op jit(solution)/shard_map/pool/pallas_call | solution.py:137
  8.3 0.0 copy-done.7
  8.4 0.0 copy-done.8
  8.4 0.0 copy-start
  8.4 0.0 copy-start.4
  8.4 17.6 %conditional.2 = (bf16[128,256]{1,0:T(8,128)(2,1)S(1)}) conditional(s32[]{:T(128)} %bitcast.3, (bf16[32,16,256]{2,1,0:T(8,128)(2,1)S(1)}, bf16[32,16,128]{2,1,0:T(8,128)(2,1)S(1)}) %tuple.18, (bf16[32,16,128]{2,1,0:T(8,128)(2,1)S(1)}, bf16[32,16,128]{2,1,0:T(8,128)(2,1)S(1)}, bf16[32,16,256]{2,1,0:T(8,128)(2,1)S(1)}, ...), branch_computations={%region_0.0_spmd, %region_1.0_spmd, %region_2.0_spmd} | conditional | flops 268435456 | bytes 7405576
  8.4 17.4 %all_to_all.22 = bf16[32,16,256]{2,1,0:T(8,128)(2,1)S(1)} all-to-all(bf16[32,16,256]{2,1,0:T(8,128)(2,1)S(1)} %get-tuple-element.30), channel_id=1, replica_groups=mesh['segment'=4,'seq'=32] {'seq'}, dimensions={0} | all-to-all | bytes 524288 | tf_op jit(solution)/shard_map/cond/branch_0_fun/all_to_all | solution.py:154
  25.8 0.2 convolution_bitcast_fusion
  26.0 0.0 copy-done
  26.0 0.0 copy-done.4
  26.0 0.0 copy-start.1
  26.1 0.4 project.1
  26.5 0.0 copy-start.3
  26.5 0.0 copy-start.5
  26.5 0.0 copy-start.6
  26.5 15.6 %all_to_all.25.got = bf16[32,4,2048]{2,1,0:T(4,128)(2,1)S(1)} all-to-all(bf16[32,4,2048]{2,1,0:T(4,128)(2,1)S(1)} %project.1), channel_id=1, replica_groups=mesh['segment'=4,'seq'=32] {'seq'}, dimensions={0} | all-to-all | bytes 1048576 | tf_op jit(solution)/shard_map/all_to_all | solution.py:346
  42.1 0.0 copy-done.1
  42.1 0.1 add_peers.1.refs_0_
  42.2 2.8 %collective-permute-start.2 = (f32[4,2048]{1,0:T(4,128)S(1)}, f32[4,2048]{1,0:T(4,128)S(1)}, u32[]{:S(2)}, u32[]{:S(2)}) collective-permute-start(f32[4,2048]{1,0:T(4,128)S(1)} %add_peers.1.refs_0_), channel_id=1, source_target_pairs={{0,96},{32,0},{64,32},{96,64},{1,97},{33,1},{65,33},{97,65},{2,98}... | collective-permute-start | bytes 98312 | tf_op jit(solution)/shard_map/ppermute | solution.py:164
  45.0 0.8 %collective-permute-start.1 = (f32[4,2048]{1,0:T(4,128)S(1)}, f32[4,2048]{1,0:T(4,128)S(1)}, u32[]{:S(2)}, u32[]{:S(2)}) collective-permute-start(f32[4,2048]{1,0:T(4,128)S(1)} %add_peers.1.refs_0_), channel_id=1, source_target_pairs={{0,64},{32,96},{64,0},{96,32},{1,65},{33,97},{65,1},{97,33},{2,66}... | collective-permute-start | bytes 98312 | tf_op jit(solution)/shard_map/ppermute | solution.py:164
  45.8 0.9 %collective-permute-start = (f32[4,2048]{1,0:T(4,128)S(1)}, f32[4,2048]{1,0:T(4,128)S(1)}, u32[]{:S(2)}, u32[]{:S(2)}) collective-permute-start(f32[4,2048]{1,0:T(4,128)S(1)} %add_peers.1.refs_0_), channel_id=1, source_target_pairs={{0,32},{32,64},{64,96},{96,0},{1,33},{33,65},{65,97},{97,1},{2,34}... | collective-permute-start | bytes 98312 | tf_op jit(solution)/shard_map/ppermute | solution.py:164
  46.7 0.1 collective-permute-done.2.refs_3_
  46.8 3.7 %collective-permute-done.1.refs_2_ = f32[4,2048]{1,0:T(4,128)S(1)} collective-permute-done((f32[4,2048]{1,0:T(4,128)S(1)}, f32[4,2048]{1,0:T(4,128)S(1)}, u32[]{:S(2)}, u32[]{:S(2)}) %collective-permute-start.1) | collective-permute-done | bytes 32800 | tf_op jit(solution)/shard_map/ppermute | solution.py:164
  50.4 0.5 collective-permute-done.refs_1_
  50.9 0.0 copy-done.3
  50.9 0.0 copy-done.5
  50.9 0.0 copy-done.6
  50.9 0.0 copy-start.2
  51.0 1.6 %make_keys.1 = (f32[4,2048]{1,0:T(4,128)S(1)}, bf16[16,128]{1,0:T(8,128)(2,1)S(1)}, bf16[16,256]{1,0:T(8,128)(2,1)S(1)}, bf16[32,16,256]{2,1,0:T(8,128)(2,1)S(1)}) custom-call(f32[4,2048]{1,0:T(4,128)S(1)} %add_peers.1.refs_0_, f32[4,2048]{1,0:T(4,128)S(1)} %collective-permute-done.refs_1_, f32[4,2048]{1,0:T(4,128)S(1)} %collective-permute-done.1.refs_2_, ...), custom_call_target="tpu_custom_call" | custom-call | tf_op jit(solution)/shard_map/make_keys/pallas_call | solution.py:294
  52.5 12.4 %all_to_all.26.got = bf16[32,16,256]{2,1,0:T(8,128)(2,1)S(1)} all-to-all(bf16[32,16,256]{2,1,0:T(8,128)(2,1)S(1)} %get-tuple-element.55), channel_id=1, replica_groups=mesh['segment'=4,'seq'=32] {'seq'}, dimensions={0} | all-to-all | bytes 524288 | tf_op jit(solution)/shard_map/all_to_all | solution.py:351
  64.9 0.0 copy-done.2
  64.9 0.8 %attend.1 = f32[4,2048]{1,0:T(4,128)S(1)} custom-call(bf16[32,16,256]{2,1,0:T(8,128)(2,1)S(1)} %all_to_all.26.got, bf16[16,128]{1,0:T(8,128)(2,1)S(1)} %get-tuple-element.56.query, bf16[16,256]{1,0:T(8,128)(2,1)S(1)} %get-tuple-element.57.own, bf16[512,2048]{1,0:T(8,128)(2,1)S(1)} %copy-done.2), custom_call_target="tpu_custom_call" | custom-call | tf_op jit(solution)/shard_map/attend/pallas_call | solution.py:313
  65.7 0.5 collective-permute-start.5
  66.2 1.3 %collective-permute-start.4 = (f32[4,2048]{1,0:T(4,128)S(1)}, f32[4,2048]{1,0:T(4,128)S(1)}, u32[]{:S(2)}, u32[]{:S(2)}) collective-permute-start(f32[4,2048]{1,0:T(4,128)S(1)} %attend.1), channel_id=1, source_target_pairs={{0,64},{32,96},{64,0},{96,32},{1,65},{33,97},{65,1},{97,33},{2,66}... | collective-permute-start | bytes 98312 | tf_op jit(solution)/shard_map/ppermute | solution.py:164
  67.5 1.2 %collective-permute-start.3 = (f32[4,2048]{1,0:T(4,128)S(1)}, f32[4,2048]{1,0:T(4,128)S(1)}, u32[]{:S(2)}, u32[]{:S(2)}) collective-permute-start(f32[4,2048]{1,0:T(4,128)S(1)} %attend.1), channel_id=1, source_target_pairs={{0,32},{32,64},{64,96},{96,0},{1,33},{33,65},{65,97},{97,1},{2,34}... | collective-permute-start | bytes 98312 | tf_op jit(solution)/shard_map/ppermute | solution.py:164
  68.7 1.3 %collective-permute-done.5 = f32[4,2048]{1,0:T(4,128)S(1)} collective-permute-done((f32[4,2048]{1,0:T(4,128)S(1)}, f32[4,2048]{1,0:T(4,128)S(1)}, u32[]{:S(2)}, u32[]{:S(2)}) %collective-permute-start.5) | collective-permute-done | bytes 32800 | tf_op jit(solution)/shard_map/ppermute | solution.py:164
  70.0 1.7 %collective-permute-done.4 = f32[4,2048]{1,0:T(4,128)S(1)} collective-permute-done((f32[4,2048]{1,0:T(4,128)S(1)}, f32[4,2048]{1,0:T(4,128)S(1)}, u32[]{:S(2)}, u32[]{:S(2)}) %collective-permute-start.4) | collective-permute-done | bytes 32800 | tf_op jit(solution)/shard_map/ppermute | solution.py:164
  71.7 0.9 %collective-permute-done.3 = f32[4,2048]{1,0:T(4,128)S(1)} collective-permute-done((f32[4,2048]{1,0:T(4,128)S(1)}, f32[4,2048]{1,0:T(4,128)S(1)}, u32[]{:S(2)}, u32[]{:S(2)}) %collective-permute-start.3) | collective-permute-done | bytes 32800 | tf_op jit(solution)/shard_map/ppermute | solution.py:164
  72.7 0.6 add_convert_fusion
Async XLA Ops:
  0.0 8.3 %copy-start.7 = (s32[4,256]{1,0:T(4,128)S(1)}, s32[4,256]{1,0:T(4,128)}, u32[]{:S(2)}) copy-start(s32[4,256]{1,0:T(4,128)} %lens.1) | copy-start | bytes 12292
  0.0 8.4 %copy-start.8 = (s32[4,256]{1,0:T(4,128)S(1)}, s32[4,256]{1,0:T(4,128)}, u32[]{:S(2)}) copy-start(s32[4,256]{1,0:T(4,128)} %secs.1) | copy-start | bytes 12292
  8.4 17.7 %copy-start = (bf16[2048,512]{1,0:T(8,128)(2,1)S(1)}, bf16[2048,512]{1,0:T(8,128)(2,1)}, u32[]{:S(2)}) copy-start(bf16[2048,512]{1,0:T(8,128)(2,1)} %refs_5_.1) | copy-start | bytes 6291460
  8.4 17.7 %copy-start.4 = (bf16[256,2048]{1,0:T(8,128)(2,1)S(1)}, bf16[256,2048]{1,0:T(8,128)(2,1)}, u32[]{:S(2)}) copy-start(bf16[256,2048]{1,0:T(8,128)(2,1)} %w_in.1) | copy-start | bytes 3145732
  26.0 16.0 %copy-start.1 = (bf16[2048,512]{1,0:T(8,128)(2,1)S(1)}, bf16[2048,512]{1,0:T(8,128)(2,1)}, u32[]{:S(2)}) copy-start(bf16[2048,512]{1,0:T(8,128)(2,1)} %refs_6_.1) | copy-start | bytes 6291460
  26.5 24.5 %copy-start.3 = (bf16[2048,512]{1,0:T(8,128)(2,1)S(1)}, bf16[2048,512]{1,0:T(8,128)(2,1)}, u32[]{:S(2)}) copy-start(bf16[2048,512]{1,0:T(8,128)(2,1)} %refs_7_.1) | copy-start | bytes 6291460
  26.5 24.4 %copy-start.5 = (f32[2048]{0:T(1024)S(1)}, f32[2048]{0:T(1024)}, u32[]{:S(2)}) copy-start(f32[2048]{0:T(1024)} %param.18) | copy-start | bytes 24580
  26.5 24.4 %copy-start.6 = (s32[4]{0:T(128)S(1)}, s32[4]{0:T(128)}, u32[]{:S(2)}) copy-start(s32[4]{0:T(128)} %refs_8_.1) | copy-start | bytes 52
  42.2 4.6 %collective-permute-start.2 = (f32[4,2048]{1,0:T(4,128)S(1)}, f32[4,2048]{1,0:T(4,128)S(1)}, u32[]{:S(2)}, u32[]{:S(2)}) collective-permute-start(f32[4,2048]{1,0:T(4,128)S(1)} %add_peers.1.refs_0_), channel_id=1, source_target_pairs={{0,96},{32,0},{64,32},{96,64},{1,97},{33,1},{65,33},{97,65},{2,98}... | collective-permute-start | bytes 98312 | tf_op jit(solution)/shard_map/ppermute | solution.py:164
  45.0 5.4 %collective-permute-start.1 = (f32[4,2048]{1,0:T(4,128)S(1)}, f32[4,2048]{1,0:T(4,128)S(1)}, u32[]{:S(2)}, u32[]{:S(2)}) collective-permute-start(f32[4,2048]{1,0:T(4,128)S(1)} %add_peers.1.refs_0_), channel_id=1, source_target_pairs={{0,64},{32,96},{64,0},{96,32},{1,65},{33,97},{65,1},{97,33},{2,66}... | collective-permute-start | bytes 98312 | tf_op jit(solution)/shard_map/ppermute | solution.py:164
  45.8 5.1 %collective-permute-start = (f32[4,2048]{1,0:T(4,128)S(1)}, f32[4,2048]{1,0:T(4,128)S(1)}, u32[]{:S(2)}, u32[]{:S(2)}) collective-permute-start(f32[4,2048]{1,0:T(4,128)S(1)} %add_peers.1.refs_0_), channel_id=1, source_target_pairs={{0,32},{32,64},{64,96},{96,0},{1,33},{33,65},{65,97},{97,1},{2,34}... | collective-permute-start | bytes 98312 | tf_op jit(solution)/shard_map/ppermute | solution.py:164
  50.9 13.9 %copy-start.2 = (bf16[512,2048]{1,0:T(8,128)(2,1)S(1)}, bf16[512,2048]{1,0:T(8,128)(2,1)}, u32[]{:S(2)}) copy-start(bf16[512,2048]{1,0:T(8,128)(2,1)} %w_out.1) | copy-start | bytes 6291460
  65.7 4.3 %collective-permute-start.5 = (f32[4,2048]{1,0:T(4,128)S(1)}, f32[4,2048]{1,0:T(4,128)S(1)}, u32[]{:S(2)}, u32[]{:S(2)}) collective-permute-start(f32[4,2048]{1,0:T(4,128)S(1)} %attend.1), channel_id=1, source_target_pairs={{0,96},{32,0},{64,32},{96,64},{1,97},{33,1},{65,33},{97,65},{2,98}... | collective-permute-start | bytes 98312 | tf_op jit(solution)/shard_map/ppermute | solution.py:164
  66.2 5.5 %collective-permute-start.4 = (f32[4,2048]{1,0:T(4,128)S(1)}, f32[4,2048]{1,0:T(4,128)S(1)}, u32[]{:S(2)}, u32[]{:S(2)}) collective-permute-start(f32[4,2048]{1,0:T(4,128)S(1)} %attend.1), channel_id=1, source_target_pairs={{0,64},{32,96},{64,0},{96,32},{1,65},{33,97},{65,1},{97,33},{2,66}... | collective-permute-start | bytes 98312 | tf_op jit(solution)/shard_map/ppermute | solution.py:164
  67.5 5.1 %collective-permute-start.3 = (f32[4,2048]{1,0:T(4,128)S(1)}, f32[4,2048]{1,0:T(4,128)S(1)}, u32[]{:S(2)}, u32[]{:S(2)}) collective-permute-start(f32[4,2048]{1,0:T(4,128)S(1)} %attend.1), channel_id=1, source_target_pairs={{0,32},{32,64},{64,96},{96,0},{1,33},{33,65},{65,97},{97,1},{2,34}... | collective-permute-start | bytes 98312 | tf_op jit(solution)/shard_map/ppermute | solution.py:164
